TPU v7x, 256 devices: a whole 4x4x8 slice. The times are simulated.
256 devices in a mesh: tok: 32 (over x, z_hi, core), hid: 8 (over y, z_lo).
Axes of the slice: x: 4, y: 4, z: 8 (z_hi: 4, z_lo: 2; z = z_hi * 2 + z_lo), core: 2. Of those that a mesh axis runs over, the one named last changes fastest.
Arguments:
- base: float32 [1024, 16384], P('tok', 'hid'), may hold values from -6 to 6
- source: float32 [1024, 16384], P('tok', 'hid'), may hold values from -6 to 6
- pairs: int32 [1024], replicated, may hold values from 0 to 1023, each once
- counts: int32 [1024], replicated, may hold values from 1 to 128
- rotation: float32 [16384, 16384], P('hid', 'tok'), may hold values from -0.046875 to 0.046875
Outputs:
- patched: float32 [1024, 16384], P('tok', 'hid')
All inputs are finite; a program needn't handle non-finite values.
Results may differ from a plain program's by a relative error of at most 0.000075.
Values sent between devices are 32-bit elements; how exact they have to be, the bound alone decides.
No kernel may reach another device: no remote copies, remote signals or barrier semaphores. Data moves between devices by JAX's collectives and lax.ppermute only.
A program may use at most 64 MiB of HBM per device.

v0:
```python
import jax
import jax.numpy as jnp
from jax import lax
from jax.sharding import PartitionSpec as P

BLOCK = 128


def local(base, source, pairs, counts, rotation):
    highest = lax.Precision.HIGHEST
    stacked = jnp.stack([base, source])
    terms = jnp.einsum(
        "srk,kc->src",
        lax.all_gather(stacked, "tok", axis=1, tiled=True),
        rotation,
        precision=highest,
        preferred_element_type=jnp.float32,
    )
    base_terms = terms[0]
    source_terms = jnp.take(terms[1], pairs, axis=0)
    width = rotation.shape[1]
    columns = lax.axis_index("tok") * width + jnp.arange(width, dtype=jnp.int32)
    summed = (
        lax.psum_scatter(base_terms, "hid", scatter_dimension=0, tiled=True),
        lax.psum_scatter(source_terms, "hid", scatter_dimension=0, tiled=True),
    )
    share = summed[0].shape[0]
    first = lax.axis_index("hid") * share
    limits = lax.dynamic_slice_in_dim(counts, first, share, 0) * BLOCK
    mixed = jnp.where(columns[None, :] < limits[:, None], summed[1], summed[0])
    full = lax.all_gather(mixed, "hid", axis=0, tiled=True)
    return lax.psum_scatter(
        lax.dot_general(
            full,
            rotation,
            (((1,), (1,)), ((), ())),
            precision=highest,
            preferred_element_type=jnp.float32,
        ),
        "tok",
        scatter_dimension=0,
        tiled=True,
    )


def solution(mesh):
    return jax.shard_map(
        local,
        mesh=mesh,
        in_specs=(P("tok", "hid"), P("tok", "hid"), P(), P(), P("hid", "tok")),
        out_specs=P("tok", "hid"),
        check_vma=False,
    )
```

profile of v0, /device:TPU:1, one launch (start us, length us, event | category | flops | bytes accessed | tf_op | source)
XLA Modules:
  0.0 485.1 jit_solution(1636365426986874242)
XLA Ops:
  6.5 0.0 all-gather.3.cloned.1.call-start
  6.5 1.9 pad_maximum_fusion
  8.4 0.0 all-gather.3.cloned.1.call-update
  8.4 0.0 reduce-scatter.4.cloned.1.call-start
  8.5 0.7 compare_and_fusion
  9.2 0.7 fusion.2
  9.9 109.6 %all-gather.3.cloned.1.call-done = f32[2,1024,2048]{2,1,0:T(8,128)} async-done(((f32[2,32,2048]{2,1,0:T(8,128)}), f32[2,1024,2048]{2,1,0:T(8,128)}) %all-gather.3.cloned.1.call-update) | async-done | bytes 16777232 | tf_op jit(solution)/shard_map/all_gather | solution.py:14
  119.4 32.0 %fusion = f32[2,1024,512]{2,1,0:T(8,128)S(1)} fusion(f32[2,1024,2048]{2,1,0:T(8,128)} %all-gather.3.cloned.1.call-done, f32[2048,512]{1,0:T(8,128)} %param.9), kind=kOutput, calls=%fused_computation.1 | convolution fusion | flops 25769803776 | bytes 25165824 | tf_op jit(solution)/shard_map/srk,kc->src/dot_general | solution.py:12
  151.4 1.8 slice_bitcast_fusion
  153.2 4.8 gather_fusion
  158.1 3.1 broadcast_select_fusion
  161.2 0.0 reduce-scatter.4.cloned.1.call-update
  161.2 0.0 reduce-scatter.6.cloned.1.call-start
  161.3 0.7 reduce-scatter.6.cloned.1.call-update
  161.9 0.0 all-gather.5.cloned.1.call-start
  162.0 0.8 dynamic-slice_multiply_fusion
  162.8 64.6 %reduce-scatter.4.cloned.1.call-done = f32[128,512]{1,0:T(8,128)} async-done(((f32[1024,512]{1,0:T(8,128)}), f32[128,512]{1,0:T(8,128)}) %reduce-scatter.4.cloned.1.call-update) | async-done | bytes 262160 | tf_op jit(solution)/shard_map/reduce_scatter | solution.py:25
  227.4 56.9 %reduce-scatter.6.cloned.1.call-done = f32[128,512]{1,0:T(8,128)} async-done(((f32[1024,512]{1,0:T(8,128)}), f32[128,512]{1,0:T(8,128)}) %reduce-scatter.6.cloned.1.call-update) | async-done | bytes 262160 | tf_op jit(solution)/shard_map/reduce_scatter | solution.py:24
  284.3 1.8 compare_select_fusion
  286.1 0.0 all-gather.5.cloned.1.call-update
  286.1 0.2 reduce-scatter.8.cloned.1.call-start
  286.4 53.8 %all-gather.5.cloned.1.call-done = f32[1024,512]{1,0:T(8,128)} async-done(((f32[128,512]{1,0:T(8,128)}), f32[1024,512]{1,0:T(8,128)}) %all-gather.5.cloned.1.call-update) | async-done | bytes 2097168 | tf_op jit(solution)/shard_map/all_gather | solution.py:31
  340.2 18.0 %fusion.3 = f32[1024,2048]{1,0:T(8,128)} fusion(f32[1024,512]{1,0:T(8,128)} %all-gather.5.cloned.1.call-done, f32[2048,512]{1,0:T(8,128)} %param.9), kind=kOutput, calls=%fused_computation.13 | convolution fusion | flops 12884901888 | bytes 14680064 | tf_op jit(solution)/shard_map/dot_general | solution.py:33
  358.2 0.0 reduce-scatter.8.cloned.1.call-update
  358.2 120.3 %reduce-scatter.8.cloned.1.call-done = f32[32,2048]{1,0:T(8,128)} async-done(((f32[1024,2048]{1,0:T(8,128)}), f32[32,2048]{1,0:T(8,128)}) %reduce-scatter.8.cloned.1.call-update) | async-done | bytes 262160 | tf_op jit(solution)/shard_map/reduce_scatter | solution.py:32
  (1 shorter events, 0.0 us)
Async XLA Ops:
  6.5 112.9 %all-gather.3.cloned.1.call-start = ((), (), s32[]{:S(2)}) async-start(), calls=%async_computation.3 | async-start | bytes 17301504 | tf_op jit(solution)/shard_map/all_gather | solution.py:14
  8.4 219.0 %reduce-scatter.4.cloned.1.call-start = ((), (), s32[]{:S(2)}) async-start(), calls=%async_computation.4 | async-start | bytes 2359296 | tf_op jit(solution)/shard_map/reduce_scatter | solution.py:25
  161.2 123.1 %reduce-scatter.6.cloned.1.call-start = ((), (), s32[]{:S(2)}) async-start(), calls=%async_computation.5 | async-start | bytes 2359296 | tf_op jit(solution)/shard_map/reduce_scatter | solution.py:24
  161.9 178.3 %all-gather.5.cloned.1.call-start = ((), (), s32[]{:S(2)}) async-start(), calls=%async_computation.6 | async-start | bytes 2359296 | tf_op jit(solution)/shard_map/all_gather | solution.py:31
  286.1 192.4 %reduce-scatter.8.cloned.1.call-start = ((), (), s32[]{:S(2)}) async-start(), calls=%async_computation.7 | async-start | bytes 8650752 | tf_op jit(solution)/shard_map/reduce_scatter | solution.py:32
Sparse Core Ops, SparseCore 0:
  10.0 109.3 all-gather.2
  161.3 66.0 reduce-scatter.3
  230.0 54.2 reduce-scatter.5
  286.3 53.9 all-gather.4
  358.3 120.1 reduce-scatter.7
where the time goes:
time: 485 us
  waiting for transfers between devices  406 us (84%)
  matrix products  50 us (10%)
  between operations  13.2 us (3%)
  other arithmetic  8.96 us (2%)
  local copies, waits for them, and re-layouts  6.63 us (1%)
    reduce_scatter x1, waiting for transfers between devices, local(): lax.psum_scatter(lax.dot_general(full, rotation, (((1,), (1,)), ((), ()))...  120 us
    all_gather x1, waiting for transfers between devices, local(): lax.all_gather(stacked, 'tok', axis=1, tiled=True)  110 us
    reduce_scatter x1, waiting for transfers between devices, local(): lax.psum_scatter(source_terms, 'hid', scatter_dimension=0, tiled=True)  64.6 us
    reduce_scatter x1, waiting for transfers between devices, local(): lax.psum_scatter(base_terms, 'hid', scatter_dimension=0, tiled=True)  56.9 us
    all_gather x1, waiting for transfers between devices, local(): full = lax.all_gather(mixed, 'hid', axis=0, tiled=True)  53.8 us
    dot_general x1, matrix products, local(): jnp.einsum('srk,kc->src', lax.all_gather(stacked, 'tok', axis=1, tiled=Tr...  32 us
    dot_general x1, matrix products, local(): lax.dot_general(full, rotation, (((1,), (1,)), ((), ())), precision=highe...  18 us
  transfers between devices with their start and end apart: 5, of which 5 were waited for; matrix products, arithmetic and copies ran while one was open for 0% of the time, Pallas kernels for 0%

commit v1 on v0

--- a/solution.py
+++ b/solution.py
@@ -28,7 +28,9 @@
     first = lax.axis_index("hid") * share
     limits = lax.dynamic_slice_in_dim(counts, first, share, 0) * BLOCK
     mixed = jnp.where(columns[None, :] < limits[:, None], summed[1], summed[0])
-    full = lax.all_gather(mixed, "hid", axis=0, tiled=True)
+    full = jnp.concatenate(
+        lax.all_to_all(jnp.stack([mixed] * lax.axis_size("hid")), "hid", 0, 0), axis=0
+    )
     return lax.psum_scatter(
         lax.dot_general(
             full,

time: 485 us -> 459 us (0.946)
  waiting for transfers between devices: 406 us -> 353 us
  blocking collectives: 0 us -> 29.5 us
    all_gather x1 -> x0, waiting for transfers between devices: 53.8 us -> none  [local(): full = lax.all_gather(mixed, 'hid', axis=0, tiled=True)]
    all_to_all x0 -> x1, blocking collectives: none -> 29.5 us  [local(): lax.all_to_all(jnp.stack([mixed] * lax.axis_size('hid')), 'hid', 0, 0)]
  transfers between devices with their start and end apart: 5 -> 4, of which waited for: 5 -> 4; matrix products, arithmetic and copies ran while one was open for 0% -> 0% of each run, Pallas kernels for 0% -> 0%
where the time goes in v1:
time: 459 us
  waiting for transfers between devices  353 us (77%)
  matrix products  47.7 us (10%)
  blocking collectives  29.5 us (6%)
  between operations  13.2 us (3%)
  other arithmetic  8.25 us (2%)
  local copies, waits for them, and re-layouts  6.9 us (2%)
    reduce_scatter x1, waiting for transfers between devices, local(): lax.psum_scatter(lax.dot_general(full, rotation, (((1,), (1,)), ((), ()))...  121 us
    all_gather x1, waiting for transfers between devices, local(): lax.all_gather(stacked, 'tok', axis=1, tiled=True)  110 us
    reduce_scatter x1, waiting for transfers between devices, local(): lax.psum_scatter(source_terms, 'hid', scatter_dimension=0, tiled=True)  64.6 us
    reduce_scatter x1, waiting for transfers between devices, local(): lax.psum_scatter(base_terms, 'hid', scatter_dimension=0, tiled=True)  56.9 us
    dot_general x1, matrix products, local(): jnp.einsum('srk,kc->src', lax.all_gather(stacked, 'tok', axis=1, tiled=Tr...  32 us
    all_to_all x1, blocking collectives, local(): lax.all_to_all(jnp.stack([mixed] * lax.axis_size('hid')), 'hid', 0, 0)  29.5 us
    dot_general x1, matrix products, local(): lax.dot_general(full, rotation, (((1,), (1,)), ((), ())), precision=highe...  15.7 us
  transfers between devices with their start and end apart: 4, of which 4 were waited for; matrix products, arithmetic and copies ran while one was open for 0% of the time, Pallas kernels for 0%

profile of v1, /device:TPU:1, one launch (start us, length us, event | category | flops | bytes accessed | tf_op | source)
XLA Modules:
  0.0 458.5 jit_solution(15458057896254739601)
XLA Ops:
  6.5 0.0 all-gather.2.cloned.1.call-start
  6.5 1.9 pad_maximum_fusion
  8.4 0.0 all-gather.2.cloned.1.call-update
  8.4 0.0 reduce-scatter.4.cloned.1.call-start
  8.5 0.7 compare_and_fusion
  9.2 0.7 fusion.2
  9.9 109.6 %all-gather.2.cloned.1.call-done = f32[2,1024,2048]{2,1,0:T(8,128)} async-done(((f32[2,32,2048]{2,1,0:T(8,128)}), f32[2,1024,2048]{2,1,0:T(8,128)}) %all-gather.2.cloned.1.call-update) | async-done | bytes 16777232 | tf_op jit(solution)/shard_map/all_gather | solution.py:14
  119.4 32.0 %fusion = f32[2,1024,512]{2,1,0:T(8,128)S(1)} fusion(f32[2,1024,2048]{2,1,0:T(8,128)} %all-gather.2.cloned.1.call-done, f32[2048,512]{1,0:T(8,128)} %param.9), kind=kOutput, calls=%fused_computation.1 | convolution fusion | flops 25769803776 | bytes 25165824 | tf_op jit(solution)/shard_map/srk,kc->src/dot_general | solution.py:12
  151.4 1.8 slice_bitcast_fusion
  153.2 4.9 %gather_fusion = f32[1024,512]{1,0:T(8,128)} fusion(f32[1024,512]{1,0:T(8,128)S(1)} %get-tuple-element.6, s32[1024]{0:T(1024)S(1)} %fusion.2), kind=kCustom, calls=%fused_computation | custom fusion | bytes 4198400 | tf_op jit(solution)/shard_map/jit(_take)/gather | solution.py:20
  158.1 3.1 broadcast_select_fusion
  161.2 0.0 reduce-scatter.4.cloned.1.call-update
  161.2 0.0 reduce-scatter.6.cloned.1.call-start
  161.3 0.7 reduce-scatter.6.cloned.1.call-update
  161.9 0.0 reduce-scatter.8.cloned.1.call-start
  162.0 0.8 dynamic-slice_multiply_fusion
  162.8 64.6 %reduce-scatter.4.cloned.1.call-done = f32[128,512]{1,0:T(8,128)} async-done(((f32[1024,512]{1,0:T(8,128)}), f32[128,512]{1,0:T(8,128)}) %reduce-scatter.4.cloned.1.call-update) | async-done | bytes 262160 | tf_op jit(solution)/shard_map/reduce_scatter | solution.py:25
  227.4 56.9 %reduce-scatter.6.cloned.1.call-done = f32[128,512]{1,0:T(8,128)} async-done(((f32[1024,512]{1,0:T(8,128)}), f32[128,512]{1,0:T(8,128)}) %reduce-scatter.6.cloned.1.call-update) | async-done | bytes 262160 | tf_op jit(solution)/shard_map/reduce_scatter | solution.py:24
  284.3 1.1 compare_select_fusion
  285.4 0.3 stack.11
  285.7 0.0 copy-start
  285.7 29.5 %all_to_all.5 = f32[8,128,512]{2,1,0:T(8,128)S(1)} all-to-all(f32[8,128,512]{2,1,0:T(8,128)S(1)} %stack.11), channel_id=1, replica_groups=mesh['tok'=32,'hid'=8] {'hid'}, dimensions={0} | all-to-all | bytes 4194304 | tf_op jit(solution)/shard_map/all_to_all | solution.py:32
  315.2 0.0 copy-done
  315.2 15.7 %fusion.3 = f32[1024,2048]{1,0:T(8,128)} fusion(f32[1024,512]{1,0:T(8,128)S(1)} %bitcast.13, f32[2048,512]{1,0:T(8,128)S(1)} %copy-done), kind=kOutput, calls=%fused_computation.13 | convolution fusion | flops 12884901888 | bytes 14680064 | tf_op jit(solution)/shard_map/dot_general | solution.py:35
  331.0 0.0 reduce-scatter.8.cloned.1.call-update
  331.0 121.0 %reduce-scatter.8.cloned.1.call-done = f32[32,2048]{1,0:T(8,128)} async-done(((f32[1024,2048]{1,0:T(8,128)}), f32[32,2048]{1,0:T(8,128)}) %reduce-scatter.8.cloned.1.call-update) | async-done | bytes 262160 | tf_op jit(solution)/shard_map/reduce_scatter | solution.py:34
  (1 shorter events, 0.0 us)
Async XLA Ops:
  6.5 112.9 %all-gather.2.cloned.1.call-start = ((), (), s32[]{:S(2)}) async-start(), calls=%async_computation.4 | async-start | bytes 17301504 | tf_op jit(solution)/shard_map/all_gather | solution.py:14
  8.4 219.0 %reduce-scatter.4.cloned.1.call-start = ((), (), s32[]{:S(2)}) async-start(), calls=%async_computation.5 | async-start | bytes 2359296 | tf_op jit(solution)/shard_map/reduce_scatter | solution.py:25
  161.2 123.1 %reduce-scatter.6.cloned.1.call-start = ((), (), s32[]{:S(2)}) async-start(), calls=%async_computation.6 | async-start | bytes 2359296 | tf_op jit(solution)/shard_map/reduce_scatter | solution.py:24
  161.9 290.0 %reduce-scatter.8.cloned.1.call-start = ((), (), s32[]{:S(2)}) async-start(), calls=%async_computation.7 | async-start | bytes 8650752 | tf_op jit(solution)/shard_map/reduce_scatter | solution.py:34
  285.7 29.5 %copy-start = (f32[2048,512]{1,0:T(8,128)S(1)}, f32[2048,512]{1,0:T(8,128)}, u32[]{:S(2)}) copy-start(f32[2048,512]{1,0:T(8,128)} %param.9) | copy-start | bytes 12582916
Sparse Core Ops, SparseCore 0:
  10.0 109.3 all-gather.1
  161.3 66.0 reduce-scatter.3
  230.0 54.2 reduce-scatter.5
  331.1 120.8 reduce-scatter.7
